TPU v7x, 32 devices: a whole 2x2x4 slice. The times are simulated.
32 devices in a mesh: groups: 2 (over y), wake: 4 (over x, core), panel: 4 (over z).
Axes of the slice: x: 2, y: 2, z: 4, core: 2. Of those that a mesh axis runs over, the one named last changes fastest.
Arguments:
- positions: float32 [3, 4096], P(None, ('groups', 'wake', 'panel')), parts along dimension 1, may hold values from -1 to 1
- strengths: float32 [3, 4096], P(None, ('groups', 'wake', 'panel')), parts along dimension 1, may hold values from -0.24 to 0.24
- cores: float32 [1, 4096], P(None, ('groups', 'wake', 'panel')), parts along dimension 1, may hold values from 0.05 to 0.2
- panel_centers: float32 [3, 32768], P(None, ('groups', 'wake', 'panel')), parts along dimension 1, may hold values from -1 to 1
- panel_normals: float32 [3, 32768], P(None, ('groups', 'wake', 'panel')), parts along dimension 1, may hold values from -1 to 1, as said below
- panel_areas: float32 [1, 32768], P(None, ('groups', 'wake', 'panel')), parts along dimension 1, may hold values from 0.004 to 0.04
- influence: float32 [32768, 16384], P(('groups', 'wake'), 'panel'), parts along dimension 0, may hold values from -1 to 2.5
- blade_ids: int32 [32768], P(('groups', 'wake', 'panel')), parts along dimension 0, may hold values from 0 to 3
- blade_velocity: float32 [8, 3], P('groups'), parts along dimension 0, may hold values from -4 to 4
Outputs:
- velocity: float32 [3, 4096], P(None, ('groups', 'wake', 'panel')), parts along dimension 1
- stretching: float32 [3, 4096], P(None, ('groups', 'wake', 'panel')), parts along dimension 1
- panel_strengths: float32 [32768], P(('groups', 'wake', 'panel')), parts along dimension 0
There are 2 independent parts, one for each index of `groups`. A program takes and returns all parts, laid end to end along the dimension named above; each array names one. Nothing has to cross between parts.
Inputs may be any that keep to these rules, and one draw needn't show every extreme that they name: `panel_normals`: each column has unit length.
All inputs are finite; a program needn't handle non-finite values.
Results may differ from a plain program's by a relative error of at most 0.0003.
Values sent between devices are 32-bit elements; how exact they have to be, the bound alone decides.
A program may use at most 128 MiB of HBM per device.

v0:
```python
import math

import jax
import jax.numpy as jnp
from jax import lax
from jax.sharding import PartitionSpec as P

BLADES = 4
ITERS = 4


inv_four_pi = 1.0 / (4.0 * math.pi)
relax_factor = 0.5
freestream = (0.0, 0.0, -1.0)
block_width = 2048


def spread(block, axis, source):
    block = jnp.where(lax.axis_index(axis) == source, block, jnp.zeros_like(block))
    return lax.psum(block, axis)


def vortex_terms(targets, sources):
    target_pos, target_str, target_core = targets
    source_pos, source_str, source_core = sources
    offset_x = target_pos[0][:, None] - source_pos[0][None, :]
    offset_y = target_pos[1][:, None] - source_pos[1][None, :]
    offset_z = target_pos[2][:, None] - source_pos[2][None, :]
    core_sq = 0.5 * (
        target_core[0][:, None] * target_core[0][:, None]
        + source_core[0][None, :] * source_core[0][None, :]
    )
    distance = offset_x * offset_x + offset_y * offset_y + offset_z * offset_z + core_sq
    inverse = lax.rsqrt(distance)
    falloff = inverse * inverse * inverse
    steeper = falloff * inverse * inverse
    source_x = source_str[0][None, :]
    source_y = source_str[1][None, :]
    source_z = source_str[2][None, :]
    target_x = target_str[0][:, None]
    target_y = target_str[1][:, None]
    target_z = target_str[2][:, None]
    cross_x = offset_y * source_z - offset_z * source_y
    cross_y = offset_z * source_x - offset_x * source_z
    cross_z = offset_x * source_y - offset_y * source_x
    twist_x = target_y * source_z - target_z * source_y
    twist_y = target_z * source_x - target_x * source_z
    twist_z = target_x * source_y - target_y * source_x
    along = 3.0 * steeper * (target_x * offset_x + target_y * offset_y + target_z * offset_z)
    return jnp.stack(
        [
            jnp.sum(falloff * cross_x, axis=1),
            jnp.sum(falloff * cross_y, axis=1),
            jnp.sum(falloff * cross_z, axis=1),
            jnp.sum(falloff * twist_x - along * cross_x, axis=1),
            jnp.sum(falloff * twist_y - along * cross_y, axis=1),
            jnp.sum(falloff * twist_z - along * cross_z, axis=1),
        ]
    )


def wake_terms(targets, sources):
    points = targets[0]
    source_pos, source_str, source_core = sources
    offset_x = points[0][:, None] - source_pos[0][None, :]
    offset_y = points[1][:, None] - source_pos[1][None, :]
    offset_z = points[2][:, None] - source_pos[2][None, :]
    distance = (
        offset_x * offset_x
        + offset_y * offset_y
        + offset_z * offset_z
        + source_core[0][None, :] * source_core[0][None, :]
    )
    inverse = lax.rsqrt(distance)
    falloff = inverse * inverse * inverse
    source_x = source_str[0][None, :]
    source_y = source_str[1][None, :]
    source_z = source_str[2][None, :]
    return jnp.stack(
        [
            jnp.sum(falloff * (offset_y * source_z - offset_z * source_y), axis=1),
            jnp.sum(falloff * (offset_z * source_x - offset_x * source_z), axis=1),
            jnp.sum(falloff * (offset_x * source_y - offset_y * source_x), axis=1),
        ]
    )


def panel_terms(targets, sources):
    points = targets[0]
    centers, weights, areas = sources
    offset_x = points[0][:, None] - centers[0][None, :]
    offset_y = points[1][:, None] - centers[1][None, :]
    offset_z = points[2][:, None] - centers[2][None, :]
    distance = (
        offset_x * offset_x + offset_y * offset_y + offset_z * offset_z + 4.0 * areas[0][None, :]
    )
    inverse = lax.rsqrt(distance)
    weighted = weights[0][None, :] * inverse * inverse * inverse
    return jnp.stack(
        [
            jnp.sum(weighted * offset_x, axis=1),
            jnp.sum(weighted * offset_y, axis=1),
            jnp.sum(weighted * offset_z, axis=1),
        ]
    )


def over_sources(kernel, targets, sources, width, out_rows):
    length = sources[0].shape[-1]
    stride = math.gcd(length, width)
    if stride == length:
        return kernel(targets, sources)
    pieces = tuple(
        (
            jnp.moveaxis(source.reshape(source.shape[0], length // stride, stride), 1, 0)
            for source in sources
        )
    )

    def visit(running, entry):
        return (running + kernel(targets, entry), None)

    initial = jnp.zeros((out_rows, targets[0].shape[-1]), jnp.float32)
    running, unused = lax.scan(visit, initial, pieces)
    return running


def column_of(row_block):
    wake_count = lax.axis_size("wake")
    panel_count = lax.axis_size("panel")
    panel_at = lax.axis_index("panel")
    first_root = panel_at * wake_count // panel_count
    donors = max(1, wake_count // panel_count)
    pieces = []
    for offset_rank in range(donors):
        pieces.append(spread(row_block, "wake", first_root + offset_rank))
    joined = pieces[0] if donors == 1 else jnp.concatenate(pieces, axis=0)
    return joined


def relax(right_side, influence):
    row_side = lax.all_gather(right_side, "panel", axis=0, tiled=True)
    current = relax_factor * row_side
    for turn in range(ITERS - 1):
        column = column_of(current)
        partial_value = jnp.dot(influence, column, precision=lax.Precision.HIGHEST)
        image = lax.psum(partial_value, "panel")
        current = current + relax_factor * (row_side - image)
    own_start = lax.axis_index("panel") * right_side.shape[0]
    return lax.dynamic_slice_in_dim(current, own_start, right_side.shape[0], 0)


def per_device(
    positions,
    strengths,
    cores,
    panel_centers,
    panel_normals,
    panel_areas,
    influence,
    blade_ids,
    blade_velocity,
):
    onset_dir = jnp.asarray(freestream, jnp.float32)[:, None]
    onehot = (blade_ids[None, :] == jnp.arange(BLADES, dtype=jnp.int32)[:, None]).astype(
        jnp.float32
    )
    kinematic = jnp.dot(blade_velocity.T, onehot, precision=lax.Precision.HIGHEST) + onset_dir
    moving = -jnp.sum(panel_normals * kinematic, axis=0)
    particles = (positions, strengths, cores)
    piece = (
        lax.all_gather(positions, ("wake", "panel"), axis=1, tiled=True),
        lax.all_gather(strengths, ("wake", "panel"), axis=1, tiled=True),
        lax.all_gather(cores, ("wake", "panel"), axis=1, tiled=True),
    )
    pair_sums = over_sources(vortex_terms, particles, piece, block_width, 6)
    wake_sums = over_sources(wake_terms, (panel_centers,), piece, block_width, 3)
    right_side = moving + inv_four_pi * jnp.sum(panel_normals * wake_sums, axis=0)
    centers, areas = (
        lax.all_gather(panel_centers, ("wake", "panel"), axis=1, tiled=True),
        lax.all_gather(panel_areas, ("wake", "panel"), axis=1, tiled=True),
    )
    panel_strengths = relax(right_side, influence)
    all_strengths = lax.all_gather(panel_strengths, ("wake", "panel"), axis=0, tiled=True)
    weights = (all_strengths * areas[0])[None, :]
    panel_sums = over_sources(panel_terms, (positions,), (centers, weights, areas), block_width, 3)
    velocity = onset_dir - inv_four_pi * pair_sums[:3] + inv_four_pi * panel_sums
    stretching = -inv_four_pi * pair_sums[3:]
    return (velocity, stretching, panel_strengths)


def solution(mesh):
    in_specs = (
        P(None, ("groups", "wake", "panel")),
        P(None, ("groups", "wake", "panel")),
        P(None, ("groups", "wake", "panel")),
        P(None, ("groups", "wake", "panel")),
        P(None, ("groups", "wake", "panel")),
        P(None, ("groups", "wake", "panel")),
        P(("groups", "wake"), "panel"),
        P(("groups", "wake", "panel")),
        P("groups", None),
    )
    out_specs = (
        P(None, ("groups", "wake", "panel")),
        P(None, ("groups", "wake", "panel")),
        P(("groups", "wake", "panel")),
    )
    return jax.shard_map(
        per_device, mesh=mesh, in_specs=in_specs, out_specs=out_specs, check_vma=False
    )
```

profile of v0, /device:TPU:3, one launch (start us, length us, event | category | flops | bytes accessed | tf_op | source)
XLA Modules:
  0.0 471.1 jit_solution(10302823508321175334)
XLA Ops:
  0.6 0.0 copy-start
  0.6 0.8 slice_bitcast_fusion.3
  1.4 29.4 %all_gather.23 = f32[3,2048]{1,0:T(4,128)S(1)} all-gather(f32[3,128]{1,0:T(4,128)} %param.13), channel_id=1, replica_groups=mesh['groups'=2,'wake'=4,'panel'=4] {'wake','panel'}, dimensions={1}, use_global_device_ids=true | all-gather | bytes 26112 | tf_op jit(solution)/shard_map/all_gather | solution.py:173
  30.9 28.5 %all_gather.21 = f32[3,2048]{1,0:T(4,128)S(1)} all-gather(f32[3,128]{1,0:T(4,128)} %param.12), channel_id=1, replica_groups=mesh['groups'=2,'wake'=4,'panel'=4] {'wake','panel'}, dimensions={1}, use_global_device_ids=true | all-gather | bytes 26112 | tf_op jit(solution)/shard_map/all_gather | solution.py:172
  59.5 30.6 %all_gather.22 = f32[1,2048]{1,0:T(1,128)S(1)} all-gather(f32[1,128]{1,0:T(1,128)} %param.14), channel_id=1, replica_groups=mesh['groups'=2,'wake'=4,'panel'=4] {'wake','panel'}, dimensions={1}, use_global_device_ids=true | all-gather | bytes 8704 | tf_op jit(solution)/shard_map/all_gather | solution.py:174
  90.1 0.7 multiply_bitcast_fusion
  90.8 2.7 fusion.43
  93.5 0.8 fusion.57
  94.4 9.8 %fusion.19 = (f32[1024]{0:T(1024)S(1)}, f32[1024]{0:T(1024)S(1)}, f32[1024]{0:T(1024)S(1)}) fusion(f32[2048]{0:T(1024)S(1)} %bitcast.113, f32[2048]{0:T(1024)S(1)} %bitcast.115, f32[2048]{0:T(1024)S(1)} %bitcast.109, f32[2048]{0:T(1024)S(1)} %bitcast.119, f32[1024]{0:T(1024)S(1)} %bitcast.124, f32[2048]{0:T(1024)S(1)} %bitcast.121, f32[1024]{0:T(1024)S(1)} %bitcast.123, ...), kind=kLoop, calls=%fused_computation.45 | loop fusion | flops 54522880 | bytes 81920 | tf_op jit(solution)/shard_map/reduce_sum | solution.py:81
  104.2 0.7 fusion.49
  105.0 0.0 copy-done
  105.0 0.9 fusion.22
  105.9 10.2 %all_gather.24 = f32[4096]{0:T(1024)S(1)} all-gather(f32[1024]{0:T(1024)S(1)} %multiply_add_fusion.2), channel_id=1, replica_groups=mesh['groups'=2,'wake'=4,'panel'=4] {'panel'}, dimensions={0}, use_global_device_ids=true | all-gather | bytes 20480 | tf_op jit(solution)/shard_map/all_gather | solution.py:142
  116.2 15.4 %psum.42 = f32[4096]{0:T(1024)S(1)} all-reduce(f32[4096]{0:T(1024)S(1)} %multiply_select_fusion), channel_id=1, replica_groups=mesh['groups'=2,'wake'=4,'panel'=4] {'wake'}, use_global_device_ids=true, to_apply=%region_8.0 | all-reduce | flops 4096 | bytes 32768 | tf_op jit(solution)/shard_map/psum | solution.py:20
  131.5 58.0 %fusion.58 = f32[1,4096]{1,0:T(1,128)S(1)} fusion(f32[4096,1]{0,1:T(1,128)S(1)} %bitcast.99, f32[4096,4096]{1,0:T(8,128)} %param.18), kind=kOutput, calls=%fused_computation.117 | convolution fusion | flops 201326592 | bytes 67141632 | tf_op jit(solution)/shard_map/dot_general | solution.py:146
  189.6 12.2 %psum.43 = f32[4096]{0:T(1024)S(1)} all-reduce(f32[4096]{0:T(1024)S(1)} %bitcast.102), channel_id=1, replica_groups=mesh['groups'=2,'wake'=4,'panel'=4] {'panel'}, use_global_device_ids=true, to_apply=%region_9.0 | all-reduce | flops 4096 | bytes 32768 | tf_op jit(solution)/shard_map/psum | solution.py:147
  201.8 13.7 %psum.44 = f32[4096]{0:T(1024)S(1)} all-reduce(f32[4096]{0:T(1024)S(1)} %fusion.50), channel_id=1, replica_groups=mesh['groups'=2,'wake'=4,'panel'=4] {'wake'}, use_global_device_ids=true, to_apply=%region_10.0 | all-reduce | flops 4096 | bytes 32768 | tf_op jit(solution)/shard_map/psum | solution.py:20
  215.5 58.0 %fusion.59 = f32[1,4096]{1,0:T(1,128)S(1)} fusion(f32[4096,1]{0,1:T(1,128)S(1)} %bitcast.100, f32[4096,4096]{1,0:T(8,128)} %param.18), kind=kOutput, calls=%fused_computation.118 | convolution fusion | flops 201326592 | bytes 67141632 | tf_op jit(solution)/shard_map/dot_general | solution.py:146
  273.5 12.3 %psum.45 = f32[4096]{0:T(1024)S(1)} all-reduce(f32[4096]{0:T(1024)S(1)} %bitcast.103), channel_id=1, replica_groups=mesh['groups'=2,'wake'=4,'panel'=4] {'panel'}, use_global_device_ids=true, to_apply=%region_11.12 | all-reduce | flops 4096 | bytes 32768 | tf_op jit(solution)/shard_map/psum | solution.py:147
  285.8 14.1 %psum.46 = f32[4096]{0:T(1024)S(1)} all-reduce(f32[4096]{0:T(1024)S(1)} %get-tuple-element.85), channel_id=1, replica_groups=mesh['groups'=2,'wake'=4,'panel'=4] {'wake'}, use_global_device_ids=true, to_apply=%region_12.13 | all-reduce | flops 4096 | bytes 32768 | tf_op jit(solution)/shard_map/psum | solution.py:20
  299.9 0.0 copy-start.4
  299.9 0.0 copy-start.2
  299.9 0.0 copy-start.1
  299.9 0.0 copy-start.5
  299.9 58.0 %fusion.60 = f32[1,4096]{1,0:T(1,128)S(1)} fusion(f32[4096,1]{0,1:T(1,128)S(1)} %bitcast.101, f32[4096,4096]{1,0:T(8,128)} %param.18), kind=kOutput, calls=%fused_computation.119 | convolution fusion | flops 201326592 | bytes 67141632 | tf_op jit(solution)/shard_map/dot_general | solution.py:146
  358.0 12.1 %psum.47 = f32[4096]{0:T(1024)S(1)} all-reduce(f32[4096]{0:T(1024)S(1)} %bitcast.104), channel_id=1, replica_groups=mesh['groups'=2,'wake'=4,'panel'=4] {'panel'}, use_global_device_ids=true, to_apply=%region_13.14 | all-reduce | flops 4096 | bytes 32768 | tf_op jit(solution)/shard_map/psum | solution.py:147
  370.0 0.0 copy-start.3
  370.1 31.0 %all_gather.25 = f32[16384]{0:T(1024)S(1)} all-gather(f32[1024]{0:T(1024)S(1)} %dynamic-slice_add_fusion), channel_id=1, replica_groups=mesh['groups'=2,'wake'=4,'panel'=4] {'wake','panel'}, dimensions={0}, use_global_device_ids=true | all-gather | bytes 69632 | tf_op jit(solution)/shard_map/all_gather | solution.py:184
  401.0 0.0 copy-done.4
  401.0 30.4 %all_gather.26 = f32[1,16384]{1,0:T(1,128)S(1)} all-gather(f32[1,1024]{1,0:T(1,128)S(1)} %copy-done.4), channel_id=1, replica_groups=mesh['groups'=2,'wake'=4,'panel'=4] {'wake','panel'}, dimensions={1}, use_global_device_ids=true | all-gather | bytes 69632 | tf_op jit(solution)/shard_map/all_gather | solution.py:181
  431.4 0.0 copy-done.2
  431.4 30.5 %all_gather.27 = f32[3,16384]{1,0:T(4,128)S(1)} all-gather(f32[3,1024]{1,0:T(4,128)S(1)} %copy-done.2), channel_id=1, replica_groups=mesh['groups'=2,'wake'=4,'panel'=4] {'wake','panel'}, dimensions={1}, use_global_device_ids=true | all-gather | bytes 208896 | tf_op jit(solution)/shard_map/all_gather | solution.py:180
  462.0 0.0 copy-done.1
  462.0 7.9 %while.11 = (s32[]{:T(128)}, f32[3,128]{1,0:T(4,128)S(1)}, f32[8,1,2048]{2,1,0:T(1,128)S(1)}, f32[3,128]{1,0:T(4,128)S(1)}, f32[8,3,2048]{2,1,0:T(4,128)S(1)}, /...) while((s32[]{:T(128)}, f32[3,128]{1,0:T(4,128)S(1)}, ...), condition=%wide.region_18.19_spmd.clone, body=%wide.region_14.0_spmd.clone.sunk | while | flops 4721797 | bytes 133791 | solution.py:124
  462.0 0.9 fusion.69
  463.0 0.9 fusion.69
  464.0 0.9 fusion.69
  465.0 0.9 fusion.69
  466.0 0.9 fusion.69
  467.0 0.9 fusion.69
  468.0 0.9 fusion.69
  469.0 0.9 fusion.69
  469.9 0.0 copy-done.5
  469.9 0.7 fusion.54
  470.5 0.6 maximum_multiply_fusion.2
  471.1 0.0 copy-done.3
  (42 shorter events, 0.7 us)
Async XLA Ops:
  0.6 104.3 %copy-start = (f32[4,3]{1,0:T(4,128)S(1)}, f32[4,3]{1,0:T(4,128)}, u32[]{:S(2)}) copy-start(f32[4,3]{1,0:T(4,128)} %param.20) | copy-start | bytes 148
  299.9 101.1 %copy-start.4 = (f32[1,1024]{1,0:T(1,128)S(1)}, f32[1,1024]{1,0:T(1,128)}, u32[]{:S(2)}) copy-start(f32[1,1024]{1,0:T(1,128)} %param.17) | copy-start | bytes 12292
  299.9 131.5 %copy-start.2 = (f32[3,1024]{1,0:T(4,128)S(1)}, f32[3,1024]{1,0:T(4,128)}, u32[]{:S(2)}) copy-start(f32[3,1024]{1,0:T(4,128)} %param.15) | copy-start | bytes 36868
  299.9 162.0 %copy-start.1 = (f32[3,128]{1,0:T(4,128)S(1)}, f32[3,128]{1,0:T(4,128)}, u32[]{:S(2)}) copy-start(f32[3,128]{1,0:T(4,128)} %param.12) | copy-start | bytes 4612
  299.9 170.0 %copy-start.5 = (f32[3]{0:T(128)S(1)}, f32[3]{0:T(128)}, u32[]{:S(2)}) copy-start(f32[3]{0:T(128)} %constant.63.clone) | copy-start | bytes 40
  370.0 101.1 %copy-start.3 = (f32[1024]{0:T(1024)}, f32[1024]{0:T(1024)S(1)}, u32[]{:S(2)}) copy-start(f32[1024]{0:T(1024)S(1)} %dynamic-slice_add_fusion) | copy-start | bytes 12292
where the time goes:
time: 477 us; the launch traced here: 471 us
  blocking collectives  270 us (57%)
  matrix products  175 us (37%)
  other arithmetic  22.8 us (5%)
    dot_general x3, matrix products, relax(): partial_value = jnp.dot(influence, column, precision=lax.Precision.HIGHEST)  174 us
    psum x3, blocking collectives, spread(): return lax.psum(block, axis)  43.1 us
    psum x3, blocking collectives, relax(): image = lax.psum(partial_value, 'panel')  36.6 us
    all_gather x1, blocking collectives, per_device(): lax.all_gather(panel_strengths, ('wake', 'panel'), axis=0, tiled=True)  31 us
    all_gather x1, blocking collectives, per_device(): lax.all_gather(cores, ('wake', 'panel'), axis=1, tiled=True)  30.6 us
    all_gather x1, blocking collectives, per_device(): lax.all_gather(panel_centers, ('wake', 'panel'), axis=1, tiled=True)  30.5 us
    all_gather x1, blocking collectives, per_device(): lax.all_gather(panel_areas, ('wake', 'panel'), axis=1, tiled=True)  30.4 us
    all_gather x1, blocking collectives, per_device(): lax.all_gather(strengths, ('wake', 'panel'), axis=1, tiled=True)  29.4 us

commit v1 on v0

v1 whole, which is shorter than its diff:
```python
import functools
import math

import jax
import jax.numpy as jnp
from jax import lax
from jax.experimental import pallas as pl
from jax.experimental.pallas import tpu as pltpu
from jax.sharding import PartitionSpec as P

ITERS = 4
PASSES = ITERS - 1
RES = 3
UNITS = 4
RING = 3
LANES = 128
MIB = 1024 * 1024

inv_four_pi = 1.0 / (4.0 * math.pi)
relax_factor = 0.5
freestream = (0.0, 0.0, -1.0)


def lane_sums(block):
    ones = jnp.ones((8, block.shape[1]), jnp.float32)
    return lax.dot_general(
        ones,
        block,
        (((1,), (1,)), ((), ())),
        precision=lax.Precision.HIGHEST,
        preferred_element_type=jnp.float32,
    )


def column(row):
    return jnp.transpose(jnp.broadcast_to(row, (row.shape[1], row.shape[1])))


def body(
    nw,
    np_,
    pos_ref,
    str_ref,
    core_ref,
    cen_ref,
    nrm_ref,
    area_ref,
    infl_ref,
    ids_ref,
    blade_ref,
    vel_ref,
    stretch_ref,
    sigma_ref,
    abuf,
    gp,
    pcol,
    tcol,
    part,
    ptab,
    wacc,
    vacc,
    wk,
    vk,
    rhs,
    rhs_col,
    xrow,
    accbuf,
    ybuf,
    ysum,
    yin,
    fin,
    tout,
    tin,
    res_sem,
    ring_sem,
    psend,
    precv,
    rsend,
    rrecv,
    ysend,
    yrecv,
    fsend,
    frecv,
    tsend,
    trecv,
):
    devices = nw * np_
    donors = nw // np_
    w = lax.axis_index("wake")
    p = lax.axis_index("panel")
    me = w * np_ + p
    rows, cols = infl_ref.shape
    own = cen_ref.shape[1]
    grp = accbuf.shape[0]
    unit = grp // UNITS
    groups = rows // grp
    ring = min(RING, groups)
    per_piece = own // grp
    local = pos_ref.shape[1]

    def peer(n):
        return {"wake": n // np_, "panel": n % np_}

    def resident(g):
        return pltpu.make_async_copy(
            infl_ref.at[pl.ds(pl.multiple_of(g * grp, grp), RES * unit), :],
            abuf.at[pl.ds(pl.multiple_of(g * RES * unit, RES * unit), RES * unit), :],
            res_sem.at[g],
        )

    def streamed(t):
        g = t % groups
        slot = t % ring
        return pltpu.make_async_copy(
            infl_ref.at[pl.ds(pl.multiple_of(g * grp + RES * unit, unit), unit), :],
            abuf.at[pl.ds(pl.multiple_of((groups * RES + slot) * unit, unit), unit), :],
            ring_sem.at[slot],
        )

    @pl.loop(0, groups)
    def _(g):
        resident(g).start()

        @pl.when(g < ring)
        def _():
            streamed(g).start()

    barrier = pltpu.get_barrier_semaphore()

    @pl.loop(1, devices)
    def _(off):
        pl.semaphore_signal(
            barrier, inc=1, device_id=peer((me + off) % devices), device_id_type=pl.DeviceIdType.MESH
        )

    mine = jnp.concatenate(
        [pos_ref[...], str_ref[...], core_ref[...], jnp.zeros((1, local), jnp.float32)], axis=0
    )
    part[me] = mine
    pl.semaphore_wait(barrier, devices - 1)

    def particle_copy(src, to):
        return pltpu.make_async_remote_copy(
            src_ref=part.at[src],
            dst_ref=part.at[src],
            send_sem=psend.at[to],
            recv_sem=precv.at[src],
            device_id=peer(to),
            device_id_type=pl.DeviceIdType.MESH,
        )

    @pl.loop(1, devices)
    def _(off):
        particle_copy(me, (me + off) % devices).start()

    for b in range(own // LANES):
        lanes = slice(b * LANES, (b + 1) * LANES)
        for d in range(3):
            pcol[d, lanes, :] = column(cen_ref[d : d + 1, lanes])
        pcol[3, lanes, :] = 4.0 * column(area_ref[0:1, lanes])
    for d in range(3):
        tcol[d] = column(pos_ref[d : d + 1, :])
        tcol[3 + d] = column(str_ref[d : d + 1, :])
    core = core_ref[0:1, :]
    tcol[6] = column(0.5 * core * core)

    @pl.loop(1, devices)
    def _(off):
        src = (me + devices - off) % devices
        particle_copy(src, src).wait_recv()

    @pl.loop(0, devices)
    def _(n):
        blk = part[n]
        px, py, pz = blk[0:1], blk[1:2], blk[2:3]
        sx, sy, sz = blk[3:4], blk[4:5], blk[5:6]
        core = blk[6:7]
        ptab[n, 0:1, :] = core * core
        ptab[n, 1:2, :] = py * sz - pz * sy
        ptab[n, 2:3, :] = pz * sx - px * sz
        ptab[n, 3:4, :] = px * sy - py * sx

    tile = 32

    @pl.loop(0, own // LANES)
    def _(b):
        @pl.loop(0, LANES // tile)
        def _(i):
            first = pl.multiple_of(b * LANES + i * tile, tile)
            here = pl.ds(first, tile)
            cx, cy, cz, ca = pcol[0, here, :], pcol[1, here, :], pcol[2, here, :], pcol[3, here, :]

            def visit(n, sums):
                dx = cx - part[n, 0:1, :]
                dy = cy - part[n, 1:2, :]
                dz = cz - part[n, 2:3, :]
                square = dx * dx + dy * dy + dz * dz
                inv = lax.rsqrt(square + ca)
                gp[n, here, :] = inv * inv * inv
                inv = lax.rsqrt(square + ptab[n, 0:1, :])
                fall = inv * inv * inv
                return (
                    sums[0] + fall * part[n, 3:4, :],
                    sums[1] + fall * part[n, 4:5, :],
                    sums[2] + fall * part[n, 5:6, :],
                    sums[3] + fall * ptab[n, 1:2, :],
                    sums[4] + fall * ptab[n, 2:3, :],
                    sums[5] + fall * ptab[n, 3:4, :],
                )

            zero = jnp.zeros((tile, LANES), jnp.float32)
            sums = lax.fori_loop(0, devices, visit, (zero,) * 6, unroll=4)
            for d in range(6):
                wacc[d, pl.ds(pl.multiple_of(i * tile, tile), tile), :] = sums[d]

        for d in range(6):
            wk[b, d : d + 1, :] = lane_sums(wacc[d])[0:1]

    for b in range(own // LANES):
        lanes = slice(b * LANES, (b + 1) * LANES)
        ids = ids_ref[0:1, lanes]
        cx, cy, cz = cen_ref[0:1, lanes], cen_ref[1:2, lanes], cen_ref[2:3, lanes]
        sx, sy, sz = wk[b, 0:1, :], wk[b, 1:2, :], wk[b, 2:3, :]
        wake = (
            cy * sz - cz * sy - wk[b, 3:4, :],
            cz * sx - cx * sz - wk[b, 4:5, :],
            cx * sy - cy * sx - wk[b, 5:6, :],
        )
        total = jnp.zeros((1, LANES), jnp.float32)
        for d in range(3):
            onset = jnp.full((1, LANES), freestream[d], jnp.float32)
            for blade in range(blade_ref.shape[0]):
                onset = onset + jnp.where(ids == blade, blade_ref[blade, d], 0.0)
            total = total + nrm_ref[d : d + 1, lanes] * (onset - inv_four_pi * wake[d])
        rhs[0:1, lanes] = -total

    holder = w // donors
    slot = w % donors

    def rhs_copy(w2, d, q):
        return pltpu.make_async_remote_copy(
            src_ref=rhs,
            dst_ref=rhs_col.at[d, q],
            send_sem=rsend.at[w2],
            recv_sem=rrecv.at[d, q],
            device_id={"wake": w2, "panel": holder},
            device_id_type=pl.DeviceIdType.MESH,
        )

    @pl.loop(0, nw)
    def _(w2):
        @pl.when(jnp.logical_or(w2 != w, holder != p))
        def _():
            rhs_copy(w2, slot, p).start()

    @pl.when(holder == p)
    def _():
        rhs_col[slot, p] = rhs[...]

    small = 16

    @pl.loop(0, local // small)
    def _(i):
        here = pl.ds(pl.multiple_of(i * small, small), small)
        tx, ty, tz = tcol[0, here, :], tcol[1, here, :], tcol[2, here, :]
        ux, uy, uz = tcol[3, here, :], tcol[4, here, :], tcol[5, here, :]
        tcore = tcol[6, here, :]

        def visit(n, sums):
            dx = tx - part[n, 0:1, :]
            dy = ty - part[n, 1:2, :]
            dz = tz - part[n, 2:3, :]
            inv = lax.rsqrt(dx * dx + dy * dy + dz * dz + (tcore + 0.5 * ptab[n, 0:1, :]))
            inv2 = inv * inv
            fall = inv2 * inv
            along = 3.0 * (fall * inv2) * (ux * dx + uy * dy + uz * dz)
            src = [part[n, 3 + d : 4 + d, :] for d in range(3)]
            src += [ptab[n, 1 + d : 2 + d, :] for d in range(3)]
            return tuple(sums[d] + fall * src[d] for d in range(6)) + tuple(
                sums[6 + d] + along * src[d] for d in range(6)
            )

        zero = jnp.zeros((small, LANES), jnp.float32)
        sums = lax.fori_loop(0, devices, visit, (zero,) * 12, unroll=4)
        for d in range(12):
            vacc[d, here, :] = sums[d]

    for d in range(12):
        vk[d : d + 1, :] = lane_sums(vacc[d])[0:1]

    @pl.loop(0, nw)
    def _(k):
        dw = p * donors + k // np_
        q = k % np_

        @pl.when(jnp.logical_or(dw != w, q != p))
        def _():
            rhs_copy(0, k // np_, q).wait_recv()

    for d in range(donors):
        for q in range(np_):
            at = (d * np_ + q) * own
            xrow[0:1, at : at + own] = relax_factor * rhs_col[d, q]

    def piece_copy(turn, piece, w2, d, q):
        return pltpu.make_async_remote_copy(
            src_ref=ybuf.at[turn, piece],
            dst_ref=yin.at[turn, d, q, piece],
            send_sem=ysend.at[turn, piece, w2],
            recv_sem=yrecv.at[turn, d, q, piece],
            device_id={"wake": w2, "panel": holder},
            device_id_type=pl.DeviceIdType.MESH,
        )

    def final_copy(piece, q):
        return pltpu.make_async_remote_copy(
            src_ref=ysum.at[piece],
            dst_ref=fin.at[q],
            send_sem=fsend.at[piece],
            recv_sem=frecv.at[q],
            device_id={"wake": w, "panel": piece},
            device_id_type=pl.DeviceIdType.MESH,
        )

    for turn in range(PASSES):
        if turn > 0:

            @pl.loop(0, nw)
            def _(k):
                d = k // np_
                q = k % np_

                @pl.when(jnp.logical_or(p * donors + d != w, q != p))
                def _():
                    @pl.loop(0, np_)
                    def _(piece):
                        piece_copy(turn - 1, piece, 0, d, q).wait_recv()

            for d in range(donors):
                for piece in range(np_):
                    at = (d * np_ + piece) * own
                    image = yin[turn - 1, d, 0, piece]
                    for q in range(1, np_):
                        image = image + yin[turn - 1, d, q, piece]
                    xrow[0:1, at : at + own] = xrow[0:1, at : at + own] + relax_factor * (
                        rhs_col[d, piece] - image
                    )

        @pl.loop(0, np_)
        def _(piece):
            @pl.loop(0, per_piece)
            def _(h):
                g = piece * per_piece + h
                t = turn * groups + g
                if turn == 0:
                    resident(g).wait()
                streamed(t).wait()

                @pl.loop(0, UNITS)
                def _(k):
                    at = jnp.where(k < RES, g * RES + k, groups * RES + t % ring)
                    at = pl.multiple_of(at * unit, unit)
                    acc = jnp.zeros((unit, LANES), jnp.float32)
                    for c in range(cols // LANES):
                        lanes = slice(c * LANES, (c + 1) * LANES)
                        acc = acc + abuf[pl.ds(at, unit), lanes] * xrow[0:1, lanes]
                    accbuf[pl.ds(pl.multiple_of(k * unit, unit), unit), :] = acc

                @pl.when(t + ring < PASSES * groups)
                def _():
                    streamed(t + ring).start()

                sums = lane_sums(accbuf[...])[0:1]
                lanes = pl.ds(pl.multiple_of(h * grp, grp), grp)
                if turn == 0:
                    ysum[piece, 0:1, lanes] = sums
                else:
                    ysum[piece, 0:1, lanes] = ysum[piece, 0:1, lanes] + sums
                if turn < PASSES - 1:
                    ybuf[turn, piece, 0:1, lanes] = sums

            if turn < PASSES - 1:

                @pl.loop(0, nw)
                def _(w2):
                    @pl.when(jnp.logical_or(w2 != w, holder != p))
                    def _():
                        piece_copy(turn, piece, w2, slot, p).start()

                @pl.when(holder == p)
                def _():
                    yin[turn, slot, p, piece] = ybuf[turn, piece]
            else:

                @pl.when(piece != p)
                def _():
                    final_copy(piece, p).start()

                @pl.when(piece == p)
                def _():
                    fin[p] = ysum[piece]

    @pl.loop(0, np_)
    def _(q):
        @pl.when(q != p)
        def _():
            final_copy(p, q).wait_recv()

    image = fin[0]
    for q in range(1, np_):
        image = image + fin[q]
    sigma = relax_factor * (ITERS * rhs[...] - image)
    sigma_ref[...] = sigma
    weights = sigma * area_ref[...]
    for b in range(own // LANES):
        lanes = slice(b * LANES, (b + 1) * LANES)
        col = column(weights[:, lanes])
        for d in range(3):
            pcol[d, lanes, :] = col * pcol[d, lanes, :]
        pcol[3, lanes, :] = col

    def sum_copy(n, src):
        return pltpu.make_async_remote_copy(
            src_ref=tout.at[n],
            dst_ref=tin.at[src],
            send_sem=tsend.at[n],
            recv_sem=trecv.at[src],
            device_id=peer(n),
            device_id_type=pl.DeviceIdType.MESH,
        )

    wide = 4

    @pl.loop(0, devices // wide)
    def _(c):
        def visit(i, sums):
            here = pl.ds(pl.multiple_of(i * 8, 8), 8)
            ws = [pcol[d, here, :] for d in (3, 0, 1, 2)]
            fresh = []
            for e in range(wide):
                fall = gp[c * wide + e, here, :]
                for d in range(4):
                    fresh.append(sums[e * 4 + d] + fall * ws[d])
            return tuple(fresh)

        zero = jnp.zeros((8, LANES), jnp.float32)
        sums = lax.fori_loop(0, own // 8, visit, (zero,) * (4 * wide), unroll=4)
        for e in range(wide):
            n = c * wide + e
            for d in range(4):
                tout[n, d : d + 1, :] = jnp.sum(sums[e * 4 + d], axis=0, keepdims=True)

            @pl.when(n != me)
            def _():
                sum_copy(n, me).start()

            @pl.when(n == me)
            def _():
                tin[me] = tout[n]

    @pl.loop(1, devices)
    def _(off):
        src = (me + devices - off) % devices
        sum_copy(src, src).wait_recv()

    pan = lax.fori_loop(1, devices, lambda n, s: s + tin[n], tin[0])
    pos = [pos_ref[d : d + 1, :] for d in range(3)]
    strn = [str_ref[d : d + 1, :] for d in range(3)]
    fs = [vk[d : d + 1, :] for d in range(3)]
    als = [vk[6 + d : 7 + d, :] for d in range(3)]
    for d in range(3):
        e, f = (d + 1) % 3, (d + 2) % 3
        pair = pos[e] * fs[f] - pos[f] * fs[e] - vk[3 + d : 4 + d, :]
        twist = strn[e] * fs[f] - strn[f] * fs[e]
        bend = pos[e] * als[f] - pos[f] * als[e] - vk[9 + d : 10 + d, :]
        panel = pos[d] * pan[0:1] - pan[1 + d : 2 + d]
        vel_ref[d : d + 1, :] = freestream[d] - inv_four_pi * pair + inv_four_pi * panel
        stretch_ref[d : d + 1, :] = -inv_four_pi * (twist - bend)

    @pl.loop(1, devices)
    def _(off):
        n = (me + off) % devices
        particle_copy(me, n).wait_send()
        sum_copy(n, me).wait_send()

    @pl.loop(0, nw)
    def _(w2):
        @pl.when(jnp.logical_or(w2 != w, holder != p))
        def _():
            rhs_copy(w2, slot, p).wait_send()
            for turn in range(PASSES - 1):

                @pl.loop(0, np_)
                def _(piece):
                    piece_copy(turn, piece, w2, slot, p).wait_send()

    @pl.loop(0, np_)
    def _(piece):
        @pl.when(piece != p)
        def _():
            final_copy(piece, p).wait_send()


def per_device(
    nw,
    np_,
    positions,
    strengths,
    cores,
    panel_centers,
    panel_normals,
    panel_areas,
    influence,
    blade_ids,
    blade_velocity,
):
    rows, cols = influence.shape
    own = panel_centers.shape[1]
    local = positions.shape[1]
    devices = nw * np_
    donors = nw // np_
    grp = min(256, own)
    unit = grp // UNITS
    groups = rows // grp
    f32 = jnp.float32
    vmem = pl.BlockSpec(memory_space=pltpu.VMEM)
    dma = pltpu.SemaphoreType.DMA
    velocity, stretching, sigma = pl.pallas_call(
        functools.partial(body, nw, np_),
        out_shape=(
            jax.ShapeDtypeStruct((3, local), f32),
            jax.ShapeDtypeStruct((3, local), f32),
            jax.ShapeDtypeStruct((1, own), f32),
        ),
        in_specs=[vmem] * 6
        + [pl.BlockSpec(memory_space=pl.ANY), vmem, pl.BlockSpec(memory_space=pltpu.SMEM)],
        out_specs=(vmem, vmem, vmem),
        scratch_shapes=[
            pltpu.VMEM(((groups * RES + RING) * unit, cols), f32),
            pltpu.VMEM((devices, own, LANES), f32),
            pltpu.VMEM((4, own, LANES), f32),
            pltpu.VMEM((7, local, LANES), f32),
            pltpu.VMEM((devices, 8, local), f32),
            pltpu.VMEM((devices, 4, local), f32),
            pltpu.VMEM((6, LANES, LANES), f32),
            pltpu.VMEM((12, local, LANES), f32),
            pltpu.VMEM((own // LANES, 8, LANES), f32),
            pltpu.VMEM((16, local), f32),
            pltpu.VMEM((1, own), f32),
            pltpu.VMEM((donors, np_, 1, own), f32),
            pltpu.VMEM((1, cols), f32),
            pltpu.VMEM((grp, LANES), f32),
            pltpu.VMEM((PASSES - 1, np_, 1, own), f32),
            pltpu.VMEM((np_, 1, own), f32),
            pltpu.VMEM((PASSES - 1, donors, np_, np_, 1, own), f32),
            pltpu.VMEM((np_, 1, own), f32),
            pltpu.VMEM((devices, 4, local), f32),
            pltpu.VMEM((devices, 4, local), f32),
            dma((groups,)),
            dma((RING,)),
            dma((devices,)),
            dma((devices,)),
            dma((nw,)),
            dma((donors, np_)),
            dma((PASSES - 1, np_, nw)),
            dma((PASSES - 1, donors, np_, np_)),
            dma((np_,)),
            dma((np_,)),
            dma((devices,)),
            dma((devices,)),
        ],
        compiler_params=pltpu.CompilerParams(
            collective_id=0, has_side_effects=True, vmem_limit_bytes=int(63.9 * MIB)
        ),
        name="rotor",
    )(
        positions,
        strengths,
        cores,
        panel_centers,
        panel_normals,
        panel_areas,
        influence,
        blade_ids.reshape(1, own),
        blade_velocity,
    )
    return velocity, stretching, sigma.reshape(own)


def solution(mesh):
    whole = P(None, ("groups", "wake", "panel"))
    line = P(("groups", "wake", "panel"))
    in_specs = (whole,) * 6 + (P(("groups", "wake"), "panel"), line, P("groups", None))
    return jax.shard_map(
        functools.partial(per_device, mesh.shape["wake"], mesh.shape["panel"]),
        mesh=mesh,
        in_specs=in_specs,
        out_specs=(whole, whole, line),
        check_vma=False,
    )
```

time: 477 us -> 83.8 us (0.18); the launches traced: 471 us -> 83.4 us
  blocking collectives: 270 us -> 0 us
  matrix products: 175 us -> 0 us
  Pallas kernels: 0 us -> 79 us
  other arithmetic: 22.8 us -> 0 us
    all_gather x7 -> x0, blocking collectives: 191 us -> none  [the longest x1 31 us: per_device(): lax.all_gather(panel_strengths, ('wake', 'panel'), axis=0, tiled=True)]
    dot_general x4 -> x0, matrix products: 175 us -> none  [the longest x3 174 us: relax(): partial_value = jnp.dot(influence, column, precision=lax.Precision.HIGHEST)]
    psum x6 -> x0, blocking collectives: 79.7 us -> none  [the longest x3 43.1 us: spread(): return lax.psum(block, axis)]
    pallas_call x0 -> x1, Pallas kernels: none -> 79 us  [per_device(): pl.pallas_call(functools.partial(body, nw, np_), out_shape=(jax.ShapeDtyp...]
    reduce_sum x11 -> x0, other arithmetic: 20.4 us -> none  [the longest x1 9.84 us: wake_terms(): jnp.sum(falloff * (offset_y * source_z - offset_z * source_y), axis=1)]
where the time goes in v1:
time: 83.8 us; the launch traced here: 83.4 us
  Pallas kernels  79 us (94%)
  local copies, waits for them, and re-layouts  3.74 us (4%)
    pallas_call x1, Pallas kernels, per_device(): pl.pallas_call(functools.partial(body, nw, np_), out_shape=(jax.ShapeDtyp...  79 us
    unnamed x3, local copies, waits for them, and re-layouts  3.74 us

profile of v1, /device:TPU:3, one launch (start us, length us, event | category | flops | bytes accessed | tf_op | source)
XLA Modules:
  0.0 83.4 jit_solution(6002714613415787229)
XLA Ops:
  0.6 79.0 %rotor.1 = (f32[3,128]{1,0:T(4,128)}, f32[3,128]{1,0:T(4,128)}, f32[1,1024]{1,0:T(1,128)}) custom-call(f32[3,128]{1,0:T(4,128)} %pos_ref.1, f32[3,128]{1,0:T(4,128)} %str_ref.1, f32[1,128]{1,0:T(1,128)} %core_ref.1, f32[3,1024]{1,0:T(4,128)} %cen_ref.1, f32[3,1024]{1,0:T(4,128)} %nrm_ref.1, f32[1,1024]{1,0:T(1,128)} %area_ref.1, f32[4096,4096]{1,0:T(8,128)} %infl_ref.1, ...), custom_call_target="tpu_custom_call" | custom-call | tf_op jit(solution)/shard_map/rotor/pallas_call | solution.py:528
  79.7 1.2 %copy.15 = f32[3,128]{1,0:T(4,128)} copy(f32[3,128]{1,0:T(4,128)} %get-tuple-element.12) | data formatting | bytes 3072
  80.9 1.2 %copy.16 = f32[3,128]{1,0:T(4,128)} copy(f32[3,128]{1,0:T(4,128)} %get-tuple-element.13) | data formatting | bytes 3072
  82.1 1.3 %copy.17 = f32[1024]{0:T(1024)} copy(f32[1024]{0:T(1024)} %bitcast.3) | data formatting | bytes 8192

commit v2 on v1

--- a/solution.py
+++ b/solution.py
@@ -22,14 +22,16 @@
 
 
 def lane_sums(block):
-    ones = jnp.ones((8, block.shape[1]), jnp.float32)
-    return lax.dot_general(
-        ones,
-        block,
-        (((1,), (1,)), ((), ())),
-        precision=lax.Precision.HIGHEST,
-        preferred_element_type=jnp.float32,
-    )
+    ones = jnp.ones((8, block.shape[1]), jnp.bfloat16)
+    total = None
+    for _ in range(3):
+        term = block.astype(jnp.bfloat16)
+        block = block - term.astype(jnp.float32)
+        sums = lax.dot_general(
+            ones, term, (((1,), (1,)), ((), ())), preferred_element_type=jnp.float32
+        )
+        total = sums if total is None else total + sums
+    return total
 
 
 def column(row):
@@ -91,7 +93,7 @@
     me = w * np_ + p
     rows, cols = infl_ref.shape
     own = cen_ref.shape[1]
-    grp = accbuf.shape[0]
+    grp = min(256, own)
     unit = grp // UNITS
     groups = rows // grp
     ring = min(RING, groups)
@@ -364,14 +366,15 @@
                     for c in range(cols // LANES):
                         lanes = slice(c * LANES, (c + 1) * LANES)
                         acc = acc + abuf[pl.ds(at, unit), lanes] * xrow[0:1, lanes]
-                    accbuf[pl.ds(pl.multiple_of(k * unit, unit), unit), :] = acc
+                    accbuf[pl.ds(pl.multiple_of(h * grp + k * unit, unit), unit), :] = acc
 
                 @pl.when(t + ring < PASSES * groups)
                 def _():
                     streamed(t + ring).start()
 
-                sums = lane_sums(accbuf[...])[0:1]
-                lanes = pl.ds(pl.multiple_of(h * grp, grp), grp)
+            for at in range(0, own, grp):
+                sums = lane_sums(accbuf[at : at + grp, :])[0:1]
+                lanes = slice(at, at + grp)
                 if turn == 0:
                     ysum[piece, 0:1, lanes] = sums
                 else:
@@ -549,7 +552,7 @@
             pltpu.VMEM((1, own), f32),
             pltpu.VMEM((donors, np_, 1, own), f32),
             pltpu.VMEM((1, cols), f32),
-            pltpu.VMEM((grp, LANES), f32),
+            pltpu.VMEM((own, LANES), f32),
             pltpu.VMEM((PASSES - 1, np_, 1, own), f32),
             pltpu.VMEM((np_, 1, own), f32),
             pltpu.VMEM((PASSES - 1, donors, np_, np_, 1, own), f32),

time: 83.8 us -> 81 us (0.967)
  Pallas kernels: 79 us -> 76 us
    pallas_call x1, Pallas kernels: 79 us -> 76 us  [per_device(): pl.pallas_call(functools.partial(body, nw, np_), out_shape=(jax.ShapeDtyp...]
where the time goes in v2:
time: 81 us; the launch traced here: 80.4 us
  Pallas kernels  76 us (94%)
  local copies, waits for them, and re-layouts  3.74 us (5%)
    pallas_call x1, Pallas kernels, per_device(): pl.pallas_call(functools.partial(body, nw, np_), out_shape=(jax.ShapeDtyp...  76 us
    unnamed x3, local copies, waits for them, and re-layouts  3.74 us

profile of v2, /device:TPU:3, one launch (start us, length us, event | category | flops | bytes accessed | tf_op | source)
XLA Modules:
  0.0 80.4 jit_solution(9963931893887134268)
XLA Ops:
  0.6 76.0 %rotor.1 = (f32[3,128]{1,0:T(4,128)}, f32[3,128]{1,0:T(4,128)}, f32[1,1024]{1,0:T(1,128)}) custom-call(f32[3,128]{1,0:T(4,128)} %pos_ref.1, f32[3,128]{1,0:T(4,128)} %str_ref.1, f32[1,128]{1,0:T(1,128)} %core_ref.1, f32[3,1024]{1,0:T(4,128)} %cen_ref.1, f32[3,1024]{1,0:T(4,128)} %nrm_ref.1, f32[1,1024]{1,0:T(1,128)} %area_ref.1, f32[4096,4096]{1,0:T(8,128)} %infl_ref.1, ...), custom_call_target="tpu_custom_call" | custom-call | tf_op jit(solution)/shard_map/rotor/pallas_call | solution.py:531
  76.7 1.2 %copy.15 = f32[3,128]{1,0:T(4,128)} copy(f32[3,128]{1,0:T(4,128)} %get-tuple-element.12) | data formatting | bytes 3072
  77.9 1.2 %copy.16 = f32[3,128]{1,0:T(4,128)} copy(f32[3,128]{1,0:T(4,128)} %get-tuple-element.13) | data formatting | bytes 3072
  79.2 1.3 %copy.17 = f32[1024]{0:T(1024)} copy(f32[1024]{0:T(1024)} %bitcast.3) | data formatting | bytes 8192
